TPU v7x, 32 devices: a whole 2x2x4 slice. The times are simulated.
32 devices in a mesh: rows: 8 (over y, x, core), kz: 4 (over z).
Axes of the slice: x: 2, y: 2, z: 4, core: 2. Of those that a mesh axis runs over, the one named last changes fastest.
Arguments:
- velocity: float32 [3, 768, 128, 512], P(None, 'rows', None, 'kz'), may hold values from -6 to 6
- forcing_blocks: bfloat16 [64, 3, 768, 256], P('kz', None, 'rows'), may hold values from -6 to 6
- mode_index: int32 [64], P('kz'), may hold values from 0 to 255
- eigen_rates: float32 [2, 384], replicated, may hold values from 0.1 to 10
- to_modes: float32 [2, 384, 384], replicated, may hold values from -1 to 2
- from_modes: float32 [2, 384, 384], replicated, may hold values from -1 to 2
Outputs:
- velocity_next: float32 [3, 768, 128, 512], P(None, None, 'rows', 'kz')
All inputs are finite; a program needn't handle non-finite values.
Results may differ from a plain program's by a relative error of at most 0.0003.
Values may be sent and summed in bfloat16 or wider, within the bound.
A program may use at most 128 MiB of HBM per device.

v0:
```python
import jax
import jax.numpy as jnp
from jax import lax
from jax.sharding import PartitionSpec as P


def shards(velocity, forcing_blocks, mode_index, eigen_rates, to_modes, from_modes):
    field_count, point_count, kx_total, column_count = velocity.shape
    mode_count = column_count // 2
    pair_count = to_modes.shape[1]
    kz_base = lax.axis_index("kz") * mode_count
    blocks = lax.all_gather(forcing_blocks, "kz", axis=0, tiled=True)
    targets = lax.all_gather(mode_index, "kz", axis=0, tiled=True)
    onehot = (
        targets[:, None] == kz_base + jnp.arange(mode_count, dtype=jnp.int32)[None, :]
    ).astype(jnp.bfloat16)
    shaped = blocks.reshape(blocks.shape[0], field_count, point_count, kx_total, 2)
    forcing = jnp.einsum("bfyxc,bm->fyxmc", shaped, onehot, preferred_element_type=jnp.float32)
    right_side = velocity + forcing.reshape(field_count, point_count, kx_total, column_count)
    row_count = lax.axis_size("rows")
    kx_local = kx_total // row_count
    kz_total = mode_count * lax.axis_size("kz")
    kz_scaled = (kz_base + jnp.arange(column_count, dtype=jnp.int32) // 2).astype(
        jnp.float32
    ) / kz_total
    exchanged = lax.all_to_all(right_side, "rows", split_axis=2, concat_axis=1, tiled=True)
    lower_half = exchanged[:, :pair_count]
    upper_half = exchanged[:, pair_count:]
    gathered = jnp.concatenate(
        [(lower_half + upper_half) * 0.5, (lower_half - upper_half) * 0.5], 1
    )
    kx_start = lax.axis_index("rows") * kx_local
    kx_scaled = (kx_start + jnp.arange(kx_local, dtype=jnp.int32)).astype(jnp.float32) / kx_total
    solved = []
    for parity_index in range(2):
        parity_block = gathered[:, parity_index * pair_count : (parity_index + 1) * pair_count]
        mode_coeff = jnp.einsum(
            "mn,fnxz->fmxz",
            to_modes[parity_index],
            parity_block,
            precision=lax.Precision.HIGHEST,
            preferred_element_type=jnp.float32,
        )
        factor = 1.0 / (
            1.0
            + eigen_rates[parity_index][:, None, None]
            + (kx_scaled**2)[None, :, None]
            + (kz_scaled**2)[None, None, :]
        )
        solved.append(
            jnp.einsum(
                "mn,fnxz->fmxz",
                from_modes[parity_index],
                mode_coeff * factor[None],
                precision=lax.Precision.HIGHEST,
                preferred_element_type=jnp.float32,
            )
        )
    return jnp.concatenate(solved, 1)


def solution(mesh):
    return jax.shard_map(
        shards,
        mesh=mesh,
        in_specs=(P(None, "rows", None, "kz"), P("kz", None, "rows", None), P("kz"), P(), P(), P()),
        out_specs=P(None, None, "rows", "kz"),
        check_vma=False,
    )
```

profile of v0, /device:TPU:0, one launch (start us, length us, event | category | flops | bytes accessed | tf_op | source)
XLA Modules:
  0.0 651.7 jit_solution(6782199726492461940)
XLA Ops:
  6.5 0.0 all-gather.2.cloned.1.call-start
  6.5 0.7 all-gather.2.cloned.1.call-update
  7.3 0.0 copy-start.5
  7.3 19.0 %copy.36 = f32[3,96,128,128]{2,1,3,0:T(8,128)} copy(f32[3,96,128,128]{3,2,1,0:T(8,128)} %param.6) | data formatting | bytes 37748736 | tf_op args[0]
  26.3 0.6 dynamic-slice
  27.5 0.0 copy-done.4
  27.6 0.2 dynamic-update-slice
  27.8 12.3 %all-reduce = s32[64]{0:T(128)S(1)} all-reduce(s32[64]{0:T(128)S(1)} %dynamic-update-slice), channel_id=1, replica_groups=mesh['rows'=8,'kz'=4] {'kz'}, use_global_device_ids=true, to_apply=%add | all-reduce | flops 64 | bytes 512
  40.1 138.5 %all-gather.2.cloned.1.call-done = bf16[64,3,96,256]{3,2,1,0:T(8,128)(2,1)} async-done(((bf16[16,3,96,256]{3,2,1,0:T(8,128)(2,1)}), bf16[64,3,96,256]{3,2,1,0:T(8,128)(2,1)}) %all-gather.2.cloned.1.call-update) | async-done | bytes 9437200 | tf_op jit(solution)/shard_map/all_gather | solution.py:12
  178.6 15.6 %copy.33 = bf16[64,3,96,256]{2,0,3,1:T(8,128)(2,1)} copy(bf16[64,3,96,256]{3,2,1,0:T(8,128)(2,1)} %all-gather.2.cloned.1.call-done) | data formatting | bytes 18874368 | tf_op jit(solution)/shard_map/all_gather | solution.py:12
  194.2 17.1 %copy.34 = bf16[64,3,96,128,2]{3,0,4,2,1:T(8,128)(2,1)} copy(bf16[64,3,96,128,2]{2,0,4,3,1:T(8,128)(2,1)} %bitcast.61) | data formatting | bytes 18874368 | tf_op jit(solution)/shard_map/reshape | solution.py:17
  211.3 12.9 %convolution_bitcast_fusion = f32[3,96,128,64,2]{2,3,4,1,0:T(8,128)} fusion(bf16[64,3,96,128,2]{3,0,4,2,1:T(8,128)(2,1)} %copy.34, s32[64]{0:T(128)S(1)} %all-reduce, s32[64]{0:T(128)S(1)} %iota_add_fusion), kind=kOutput, calls=%fused_computation.11 | convolution fusion | flops 603983872 | bytes 28312064 | tf_op jit(solution)/shard_map/bfyxc,bm->fyxmc/dot_general | solution.py:18
  224.2 19.9 %copy.35 = f32[3,96,128,64,2]{2,1,4,3,0:T(8,128)} copy(f32[3,96,128,64,2]{2,3,4,1,0:T(8,128)} %convolution_bitcast_fusion) | data formatting | bytes 37748736 | tf_op jit(solution)/shard_map/bfyxc,bm->fyxmc/transpose | solution.py:18
  244.1 0.0 slice-done.3
  244.1 0.0 slice-done.4
  244.2 15.7 %add.132 = f32[3,96,128,128]{2,1,3,0:T(8,128)} add(f32[3,96,128,128]{2,1,3,0:T(8,128)S(1)} %bitcast.58, f32[3,96,128,128]{2,1,3,0:T(8,128)} %bitcast.59) | non-fusion elementwise | flops 4718592 | bytes 56623104 | tf_op jit(solution)/shard_map/add | solution.py:19
  259.9 18.8 %copy.37 = f32[3,96,128,128]{3,1,0,2:T(8,128)} copy(f32[3,96,128,128]{2,1,3,0:T(8,128)} %add.132) | data formatting | bytes 37748736 | tf_op jit(solution)/shard_map/add | solution.py:19
  278.7 6.3 all-to-all-start
  285.1 0.1 broadcast_add_fusion.1
  285.1 2.5 add_divide_fusion.1
  287.6 203.8 %all-to-all-done = f32[3,96,128,128]{3,1,0,2:T(8,128)} async-done(((f32[3,96,128,128]{3,1,0,2:T(8,128)}), f32[3,96,128,128]{3,1,0,2:T(8,128)}, u32[]{:S(2)}, u32[]{:S(2)}) %all-to-all-start) | async-done | bytes 18874400 | tf_op jit(solution)/shard_map/all_to_all | solution.py:26
  491.4 17.8 %copy.39 = f32[3,8,96,16,128]{4,3,2,1,0:T(8,128)S(1)} copy(f32[3,8,96,16,128]{4,2,0,3,1:T(8,128)} %bitcast.8) | data formatting | bytes 37748736 | tf_op jit(solution)/shard_map/all_to_all | solution.py:26
  509.2 4.2 add_multiply_fusion
  513.4 35.2 %fusion.4 = f32[3,16,128,384]{3,2,1,0:T(8,128)S(1)} fusion(f32[3,384,16,128]{3,2,1,0:T(8,128)} %get-tuple-element.7, f32[2,384,384]{2,1,0:T(8,128)} %param.10), kind=kOutput, calls=%fused_computation.7 | convolution fusion | flops 10871635968 | bytes 19464192 | tf_op jit(solution)/shard_map/mn,fnxz->fmxz/dot_general | solution.py:37
  548.6 0.0 copy-done.1
  548.6 0.0 copy-start
  548.6 33.0 %fusion.2 = f32[3,16,128,384]{3,2,1,0:T(8,128)S(1)} fusion(f32[3,384,16,128]{3,2,1,0:T(8,128)S(1)} %get-tuple-element.8, f32[2,384,384]{2,1,0:T(8,128)S(1)} %copy-done.1), kind=kOutput, calls=%fused_computation.5 | convolution fusion | flops 10871635968 | bytes 19464192 | tf_op jit(solution)/shard_map/mn,fnxz->fmxz/dot_general | solution.py:37
  581.6 0.0 copy-start.2
  581.7 19.2 %fusion.8 = f32[3,384,16,128]{1,3,2,0:T(8,128)S(1)} fusion(f32[3,16,128,384]{3,2,1,0:T(8,128)S(1)} %fusion.4, f32[384,16,128]{0,2,1:T(8,128)S(1)} %copy-done, f32[2,384,384]{2,1,0:T(8,128)} %param.11), kind=kOutput, calls=%fused_computation.14 | convolution fusion | flops 10873995264 | bytes 22609920 | tf_op jit(solution)/shard_map/mn,fnxz->fmxz/dot_general | solution.py:51
  600.8 18.0 %fusion.9 = f32[3,384,16,128]{1,3,2,0:T(8,128)S(1)} fusion(f32[3,16,128,384]{3,2,1,0:T(8,128)S(1)} %fusion.2, f32[384,16,128]{0,2,1:T(8,128)S(1)} %get-tuple-element.10, f32[2,384,384]{2,1,0:T(8,128)S(1)} %copy-done.2), kind=kOutput, calls=%fused_computation.15 | convolution fusion | flops 10873995264 | bytes 22609920 | tf_op jit(solution)/shard_map/mn,fnxz->fmxz/dot_general | solution.py:51
  618.9 6.9 %pad_maximum_fusion = f32[3,768,16,128]{1,3,2,0:T(8,128)} fusion(f32[3,384,16,128]{1,3,2,0:T(8,128)S(1)} %fusion.9, f32[3,384,16,128]{1,3,2,0:T(8,128)S(1)} %fusion.8), kind=kLoop, calls=%fused_computation | loop fusion | flops 4718592 | bytes 37748736 | tf_op jit(solution)/shard_map/concatenate | solution.py:59
  625.8 18.7 %copy.42 = f32[3,768,16,128]{3,2,1,0:T(8,128)} copy(f32[3,768,16,128]{1,3,2,0:T(8,128)} %pad_maximum_fusion) | data formatting | bytes 37748736 | tf_op jit(solution)/shard_map/concatenate | solution.py:59
  (21 shorter events, 0.1 us)
Async XLA Ops:
  6.5 172.1 %all-gather.2.cloned.1.call-start = ((), (), s32[]{:S(2)}) async-start(), calls=%async_computation.1 | async-start | bytes 11796480 | tf_op jit(solution)/shard_map/all_gather | solution.py:12
  7.3 19.0 %copy-start.5 = (u32[32]{0:T(128)S(1)}, u32[32]{0:T(128)}, u32[]{:S(2)}) copy-start(u32[32]{0:T(128)} %constant.42) | copy-start | bytes 388
  7.3 20.3 %copy-start.4 = (s32[16]{0:T(128)S(1)}, s32[16]{0:T(128)}, u32[]{:S(2)}) copy-start(s32[16]{0:T(128)} %param.8) | copy-start | bytes 196
  211.3 32.8 %slice-start = ((s8[18874368]{0:T(1024)(128)(4,1)}), s8[4194304]{0:T(1024)(128)(4,1)S(1)}, s32[]{:S(2)}) async-start(s8[18874368]{0:T(1024)(128)(4,1)} %bitcast.57), calls=%async_computation.2 | async-start | bytes 8388608
  211.3 32.8 %slice-start.1 = ((s8[18874368]{0:T(1024)(128)(4,1)}), s8[4194304]{0:T(1024)(128)(4,1)S(1)}, s32[]{:S(2)}) async-start(s8[18874368]{0:T(1024)(128)(4,1)} %bitcast.57), calls=%async_computation.3 | async-start | bytes 8388608
  211.3 32.8 %slice-start.2 = ((s8[18874368]{0:T(1024)(128)(4,1)}), s8[2097152]{0:T(1024)(128)(4,1)S(1)}, s32[]{:S(2)}) async-start(s8[18874368]{0:T(1024)(128)(4,1)} %bitcast.57), calls=%async_computation.4 | async-start | bytes 4194304
  224.2 19.9 %slice-start.3 = ((s8[18874368]{0:T(1024)(128)(4,1)}), s8[4194304]{0:T(1024)(128)(4,1)S(1)}, s32[]{:S(2)}) async-start(s8[18874368]{0:T(1024)(128)(4,1)} %bitcast.57), calls=%async_computation.5 | async-start | bytes 8388608
  224.2 19.9 %slice-start.4 = ((s8[18874368]{0:T(1024)(128)(4,1)}), s8[4194304]{0:T(1024)(128)(4,1)S(1)}, s32[]{:S(2)}) async-start(s8[18874368]{0:T(1024)(128)(4,1)} %bitcast.57), calls=%async_computation.6 | async-start | bytes 8388608
  278.7 6.3 copy-start.3
  278.7 212.7 %all-to-all-start = ((f32[3,96,128,128]{3,1,0,2:T(8,128)}), f32[3,96,128,128]{3,1,0,2:T(8,128)}, u32[]{:S(2)}, u32[]{:S(2)}) async-start(f32[3,96,128,128]{3,1,0,2:T(8,128)} %copy.37), calls=%async_computation | async-start | bytes 37748736 | tf_op jit(solution)/shard_map/all_to_all | solution.py:26
  513.4 35.2 %copy-start.1 = (f32[2,384,384]{2,1,0:T(8,128)S(1)}, f32[2,384,384]{2,1,0:T(8,128)}, u32[]{:S(2)}) copy-start(f32[2,384,384]{2,1,0:T(8,128)} %param.10) | copy-start | bytes 3538948
  548.6 33.1 %copy-start = (f32[384,16,128]{0,2,1:T(8,128)S(1)}, f32[384,16,128]{0,2,1:T(8,128)}, u32[]{:S(2)}) copy-start(f32[384,16,128]{0,2,1:T(8,128)} %get-tuple-element.9) | copy-start | bytes 9437188
  581.6 19.2 %copy-start.2 = (f32[2,384,384]{2,1,0:T(8,128)S(1)}, f32[2,384,384]{2,1,0:T(8,128)}, u32[]{:S(2)}) copy-start(f32[2,384,384]{2,1,0:T(8,128)} %param.11) | copy-start | bytes 3538948
Sparse Core Ops, SparseCore 0:
  8.9 169.6 all-gather.1
where the time goes:
time: 661 us; the launch traced here: 652 us
  waiting for transfers between devices  343 us (52%)
  local copies, waits for them, and re-layouts  128 us (19%)
  matrix products  118 us (18%)
  other arithmetic  29.4 us (4%)
  between operations  14.6 us (2%)
  blocking collectives  12.3 us (2%)
    all_to_all x1, waiting for transfers between devices, shards(): lax.all_to_all(right_side, 'rows', split_axis=2, concat_axis=1, tiled=True)  204 us
    all_gather x1, waiting for transfers between devices, shards(): blocks = lax.all_gather(forcing_blocks, 'kz', axis=0, tiled=True)  138 us
    dot_general x2, matrix products, shards(): jnp.einsum('mn,fnxz->fmxz', to_modes[parity_index], parity_block, precisi...  68.2 us
    dot_general x2, matrix products, shards(): jnp.einsum('mn,fnxz->fmxz', from_modes[parity_index], mode_coeff * factor...  37.2 us
    unnamed x26, local copies, waits for them, and re-layouts  19.9 us
    transpose x1, local copies, waits for them, and re-layouts, shards(): jnp.einsum('bfyxc,bm->fyxmc', shaped, onehot, preferred_element_type=jnp....  19.9 us
    add x1, local copies, waits for them, and re-layouts, shards(): velocity + forcing.reshape(field_count, point_count, kx_total, column_count)  18.8 us
    concatenate x1, local copies, waits for them, and re-layouts, shards(): return jnp.concatenate(solved, 1)  18.7 us
  transfers between devices with their start and end apart: 2, of which 2 were waited for; matrix products, arithmetic and copies ran while one was open for 3% of the time, Pallas kernels for 0%

commit v1 on v0

v1 whole, which is shorter than its diff:
```python
import functools
import math

import jax
import jax.numpy as jnp
from jax import lax
from jax.experimental import pallas as pl
from jax.experimental.pallas import tpu as pltpu
from jax.sharding import PartitionSpec as P

F32 = jnp.float32
BF16 = jnp.bfloat16
S16 = jnp.int16
FLOOR = 1e-5


def code_steps(bound):
    return 32760.0 / math.log1p(bound / FLOOR)


def encode(value, steps):
    size = steps * jnp.log(1.0 + jnp.abs(value) * (1.0 / FLOOR)) + 0.5
    return jnp.where(value < 0.0, -size, size).astype(jnp.int32).astype(S16)


def decode(code, steps, gain):
    level = code.astype(jnp.int32).astype(F32) * (1.0 / steps)
    size = (jnp.exp(jnp.abs(level)) - 1.0) * (FLOOR * gain)
    return jnp.where(level < 0.0, -size, size)


def spread_kernel(steps, velocity_ref, blocks_ref, onehot_ref, out_ref):
    onehot = onehot_ref[...]
    for y in range(velocity_ref.shape[1]):
        block = blocks_ref[:, y].reshape(onehot.shape[0], blocks_ref.shape[3])
        forcing = lax.dot_general(
            block, onehot, (((0,), (0,)), ((), ())), preferred_element_type=F32
        )
        code = encode(velocity_ref[0, y] + forcing, steps)
        out_ref[:, y] = code.reshape(out_ref.shape[0], out_ref.shape[2], out_ref.shape[3])


def spread(component, velocity, blocks, onehot, row_count, steps, step):
    _, y_count, x_count, z_count = velocity.shape
    x_local = x_count // row_count
    return pl.pallas_call(
        functools.partial(spread_kernel, steps),
        grid=(y_count // step,),
        in_specs=[
            pl.BlockSpec((1, step, x_count, z_count), lambda i: (component, i, 0, 0)),
            pl.BlockSpec(
                (blocks.shape[0], step) + blocks.shape[2:], lambda i: (0, i, 0, 0)
            ),
            pl.BlockSpec(onehot.shape, lambda i: (0, 0)),
        ],
        out_specs=pl.BlockSpec((row_count, step, x_local, z_count), lambda i: (0, i, 0, 0)),
        out_shape=jax.ShapeDtypeStruct((row_count, y_count, x_local, z_count), S16),
        compiler_params=pltpu.CompilerParams(vmem_limit_bytes=40 * 2**20),
        cost_estimate=pl.CostEstimate(
            flops=2 * y_count * x_count * z_count * onehot.shape[0],
            bytes_accessed=y_count * x_count * z_count * 6 + blocks.size * 2,
            transcendentals=0,
        ),
    )(velocity, blocks, onehot)


def split(value):
    high = value.astype(BF16)
    low = (value - high.astype(F32)).astype(BF16)
    return high, low


def weights_of(value):
    high, low = split(value)
    return jnp.concatenate([high, high, low], 1)


def product(weights, value):
    high, low = split(value)
    return jnp.dot(weights, jnp.concatenate([high, low, high], 0), preferred_element_type=F32)


def solve_kernel(steps, width, values_ref, rates_ref, shifts_ref, to_ref, from_ref, *rest):
    out_ref, folded = rest[-2:]
    pair_count = to_ref.shape[1]
    x_count, z_count = shifts_ref.shape
    sign = jnp.where(pl.program_id(0) == 0, 1.0, -1.0).astype(F32)
    chunk = 16

    @pl.loop(0, pair_count // chunk)
    def _(i):
        rows = pl.ds(pl.multiple_of(i * chunk, chunk), chunk)
        uppers = pl.ds(pl.multiple_of(pair_count + i * chunk, chunk), chunk)
        lower = decode(values_ref[rows], steps, 0.5)
        upper = decode(values_ref[uppers], steps, 0.5)
        target = pl.ds(pl.multiple_of(i * chunk * x_count, chunk * x_count), chunk * x_count)
        folded[target] = (lower + sign * upper).reshape(chunk * x_count, z_count)

    to_weights = weights_of(to_ref[0])
    from_weights = weights_of(from_ref[0])
    rates = rates_ref[0]
    for start in range(0, x_count, width):
        columns = range(start, start + width)
        value = jnp.concatenate(
            [folded[pl.ds(x, pair_count, stride=x_count), :] for x in columns], 1
        )
        coeff = product(to_weights, value)
        shift = jnp.concatenate([shifts_ref[x : x + 1, :] for x in columns], 1)
        solved = product(from_weights, coeff * (1.0 / (rates + shift)))
        for k, x in enumerate(columns):
            out_ref[pl.ds(x, pair_count, stride=x_count), :] = solved[
                :, k * z_count : (k + 1) * z_count
            ]


def solve(component, field_count, values, rates, shifts, to_modes, from_modes, previous, steps):
    point_count, x_count, z_count = values.shape
    pair_count = point_count // 2
    specs = [
        pl.BlockSpec(values.shape, lambda p: (0, 0, 0)),
        pl.BlockSpec((1, pair_count, 1), lambda p: (p, 0, 0)),
        pl.BlockSpec(shifts.shape, lambda p: (0, 0)),
        pl.BlockSpec((1, pair_count, pair_count), lambda p: (p, 0, 0)),
        pl.BlockSpec((1, pair_count, pair_count), lambda p: (p, 0, 0)),
    ]
    operands = [values, rates, shifts, to_modes, from_modes]
    aliases = {}
    if previous is not None:
        aliases = {len(operands): 0}
        specs.append(pl.BlockSpec(memory_space=pl.ANY))
        operands.append(previous)
    return pl.pallas_call(
        functools.partial(solve_kernel, steps, 4),
        grid=(2,),
        in_specs=specs,
        out_specs=pl.BlockSpec(
            (pair_count * x_count, z_count), lambda p: (component * 2 + p, 0)
        ),
        out_shape=jax.ShapeDtypeStruct((field_count * point_count * x_count, z_count), F32),
        scratch_shapes=[pltpu.VMEM((pair_count * x_count, z_count), F32)],
        input_output_aliases=aliases,
        compiler_params=pltpu.CompilerParams(vmem_limit_bytes=48 * 2**20),
        cost_estimate=pl.CostEstimate(
            flops=12 * point_count * pair_count * x_count * z_count,
            bytes_accessed=values.size * 6,
            transcendentals=0,
        ),
    )(*operands)


def shards(velocity, forcing_blocks, mode_index, eigen_rates, to_modes, from_modes):
    field_count, y_count, kx_total, column_count = velocity.shape
    mode_count = column_count // 2
    row_count = lax.axis_size("rows")
    kz_count = lax.axis_size("kz")
    kx_local = kx_total // row_count
    block_count = forcing_blocks.shape[0]
    bound = 6.0 * (block_count * kz_count + 1)
    steps = code_steps(bound)

    kz_base = lax.axis_index("kz") * mode_count
    lanes = jnp.arange(2 * kx_total, dtype=jnp.int32)
    swap = (
        lanes[:, None] == (lanes % kx_total * 2 + lanes // kx_total)[None, :]
    ).astype(BF16)
    parts = jnp.einsum("bcyk,kl->cybl", forcing_blocks, swap, preferred_element_type=BF16)
    parts = parts.reshape(field_count, y_count, 2 * block_count, kx_total)
    targets = lax.all_gather(mode_index, "kz", axis=0, tiled=True)
    columns = jnp.arange(column_count, dtype=jnp.int32)
    keys = (2 * targets[:, None] + jnp.arange(2, dtype=jnp.int32)[None, :]).reshape(-1)
    onehot = (keys[:, None] == (2 * kz_base + columns)[None, :]).astype(BF16)

    kz_total = mode_count * kz_count
    kz_scaled = (kz_base + columns // 2).astype(F32) / kz_total
    kx_start = lax.axis_index("rows") * kx_local
    kx_scaled = (kx_start + jnp.arange(kx_local, dtype=jnp.int32)).astype(F32) / kx_total
    shifts = 1.0 + (kx_scaled**2)[:, None] + (kz_scaled**2)[None, :]
    rates = eigen_rates[:, :, None]

    result = None
    for component in range(field_count):
        blocks = lax.all_gather(parts[component], "kz", axis=0, tiled=False)
        sent = spread(component, velocity, blocks, onehot, row_count, steps, 16)
        values = lax.all_to_all(sent, "rows", split_axis=0, concat_axis=0, tiled=True)
        values = values.reshape(row_count * y_count, kx_local, column_count)
        result = solve(
            component, field_count, values, rates, shifts, to_modes, from_modes, result, steps
        )
    return result.reshape(field_count, row_count * y_count, kx_local, column_count)


def solution(mesh):
    return jax.shard_map(
        shards,
        mesh=mesh,
        in_specs=(P(None, "rows", None, "kz"), P("kz", None, "rows", None), P("kz"), P(), P(), P()),
        out_specs=P(None, None, "rows", "kz"),
        check_vma=False,
    )
```

time: 661 us -> 294 us (0.44); the launches traced: 652 us -> 293 us
  waiting for transfers between devices: 343 us -> 146 us
  matrix products: 118 us -> 0.79 us
  local copies, waits for them, and re-layouts: 128 us -> 29.3 us
  Pallas kernels: 0 us -> 80.2 us
  other arithmetic: 29.4 us -> 0.26 us
    all_to_all x1 -> x3, waiting for transfers between devices: 204 us -> 0.01 us  [shards(): lax.all_to_all(sent, 'rows', split_axis=0, concat_axis=0, tiled=True)]
    dot_general x5 -> x1, matrix products: 118 us -> 0.79 us  [shards(): jnp.einsum('bcyk,kl->cybl', forcing_blocks, swap, preferred_element_type=...]
    pallas_call x0 -> x6, Pallas kernels: none -> 80.2 us  [the longest x3 58.6 us: solve(): pl.pallas_call(functools.partial(solve_kernel, steps, 4), grid=(2,), in_s...]
    transpose x1 -> x0, local copies, waits for them, and re-layouts: 19.9 us -> none  [shards(): jnp.einsum('bfyxc,bm->fyxmc', shaped, onehot, preferred_element_type=jnp....]
    concatenate x1 -> x0, local copies, waits for them, and re-layouts: 18.7 us -> none  [shards(): return jnp.concatenate(solved, 1)]
    add x1, local copies, waits for them, and re-layouts: 18.8 us -> 0.14 us  [shards(): 2 * targets[:, None] + jnp.arange(2, dtype=jnp.int32)[None, :]]
    all_to_all x1 -> x0, local copies, waits for them, and re-layouts: 17.8 us -> none  [shards(): lax.all_to_all(right_side, 'rows', split_axis=2, concat_axis=1, tiled=True)]
    reshape x1 -> x0, local copies, waits for them, and re-layouts: 17.1 us -> none  [shards(): blocks.reshape(blocks.shape[0], field_count, point_count, kx_total, 2)]
  transfers between devices with their start and end apart: 2 -> 6, of which waited for: 2 -> 3; matrix products, arithmetic and copies ran while one was open for 3% -> 3% of each run, Pallas kernels for 0% -> 20%
where the time goes in v1:
time: 294 us; the launch traced here: 293 us
  waiting for transfers between devices  146 us (50%)
  Pallas kernels  80.2 us (27%)
  local copies, waits for them, and re-layouts  29.3 us (10%)
  between operations  14 us (5%)
  starting transfers between devices  12.1 us (4%)
  blocking collectives  9.89 us (3%)
    all_gather x3, waiting for transfers between devices, shards(): blocks = lax.all_gather(parts[component], 'kz', axis=0, tiled=False)  146 us
    pallas_call x3, Pallas kernels, solve(): pl.pallas_call(functools.partial(solve_kernel, steps, 4), grid=(2,), in_s...  58.6 us
    pallas_call x3, Pallas kernels, spread(): pl.pallas_call(functools.partial(spread_kernel, steps), grid=(y_count //...  21.6 us
    unnamed x35, local copies, waits for them, and re-layouts  20.2 us
    all_to_all x3, starting transfers between devices, shards(): lax.all_to_all(sent, 'rows', split_axis=0, concat_axis=0, tiled=True)  12.1 us
    unnamed x1, blocking collectives  9.89 us
    slice x7, local copies, waits for them, and re-layouts, shards(): blocks = lax.all_gather(parts[component], 'kz', axis=0, tiled=False)  8.77 us
  transfers between devices with their start and end apart: 6, of which 3 were waited for; matrix products, arithmetic and copies ran while one was open for 3% of the time, Pallas kernels for 20%

profile of v1, /device:TPU:0, one launch (start us, length us, event | category | flops | bytes accessed | tf_op | source)
XLA Modules:
  0.0 293.1 jit_solution(5329073284051830821)
XLA Ops:
  6.5 1.7 copy-done
  8.2 0.8 convolution_bitcast_fusion
  9.0 1.0 fusion.11
  10.5 1.1 slice.23
  12.2 1.1 slice.21
  13.3 0.7 dynamic-slice
  15.0 9.9 %all-reduce = s32[64]{0:T(128)S(1)} all-reduce(s32[64]{0:T(128)S(1)} %dynamic-update-slice), channel_id=1, replica_groups=mesh['rows'=8,'kz'=4] {'kz'}, use_global_device_ids=true, to_apply=%add | all-reduce | flops 64 | bytes 512
  25.2 52.8 %all-gather.8.cloned.1.call-done.blocks_ref = bf16[4,96,32,128]{3,2,1,0:T(8,128)(2,1)} async-done(((bf16[1,96,32,128]{3,2,1,0:T(8,128)(2,1)}), bf16[4,96,32,128]{3,2,1,0:T(8,128)(2,1)}) %all-gather.8.cloned.1.call-update) | async-done | bytes 3145744 | tf_op jit(solution)/shard_map/all_gather | solution.py:182
  78.0 1.9 copy-done.9
  79.9 8.0 %shard_map.66 = s16[8,96,16,128]{3,2,1,0:T(8,128)(2,1)} custom-call(f32[3,96,128,128]{3,2,1,0:T(8,128)} %velocity_ref.5, bf16[4,96,32,128]{3,2,1,0:T(8,128)(2,1)S(1)} %copy-done.9, bf16[128,128]{1,0:T(8,128)(2,1)S(1)} %compare_convert_fusion.onehot_ref), custom_call_target="tpu_custom_call" | custom-call | flops 402653184 | bytes 12582912 | tf_op jit(solution)/shard_map/pallas_call | solution.py:46
  87.9 3.6 %all-to-all-start.2 = ((s16[8,96,16,128]{3,2,1,0:T(8,128)(2,1)}), s16[8,96,16,128]{3,2,1,0:T(8,128)(2,1)S(1)}, u32[]{:S(2)}, u32[]{:S(2)}) async-start(s16[8,96,16,128]{3,2,1,0:T(8,128)(2,1)} %shard_map.66), calls=%async_computation.2 | async-start | bytes 6291456 | tf_op jit(solution)/shard_map/all_to_all | solution.py:184
  91.6 2.5 copy.21
  94.1 2.1 slice.19
  96.2 45.5 %all-gather.6.cloned.1.call-done.blocks_ref = bf16[4,96,32,128]{3,2,1,0:T(8,128)(2,1)} async-done(((bf16[1,96,32,128]{3,2,1,0:T(8,128)(2,1)}), bf16[4,96,32,128]{3,2,1,0:T(8,128)(2,1)}) %all-gather.6.cloned.1.call-update) | async-done | bytes 3145744 | tf_op jit(solution)/shard_map/all_gather | solution.py:182
  141.8 1.9 copy-done.8
  143.7 6.9 %shard_map.65 = s16[8,96,16,128]{3,2,1,0:T(8,128)(2,1)S(1)} custom-call(f32[3,96,128,128]{3,2,1,0:T(8,128)} %velocity_ref.5, bf16[4,96,32,128]{3,2,1,0:T(8,128)(2,1)S(1)} %copy-done.8, bf16[128,128]{1,0:T(8,128)(2,1)S(1)} %compare_convert_fusion.onehot_ref), custom_call_target="tpu_custom_call" | custom-call | flops 402653184 | bytes 12582912 | tf_op jit(solution)/shard_map/pallas_call | solution.py:46
  150.5 1.7 copy-done.3
  152.2 1.6 copy-done.11
  153.8 3.7 %all-to-all-start.1 = ((s16[8,96,16,128]{3,2,1,0:T(8,128)(2,1)}), s16[8,96,16,128]{3,2,1,0:T(8,128)(2,1)S(1)}, u32[]{:S(2)}, u32[]{:S(2)}) async-start(s16[8,96,16,128]{3,2,1,0:T(8,128)(2,1)} %copy-done.3), calls=%async_computation.1 | async-start | bytes 6291456 | tf_op jit(solution)/shard_map/all_to_all | solution.py:184
  157.5 48.0 %all-gather.4.cloned.1.call-done.blocks_ref = bf16[4,96,32,128]{3,2,1,0:T(8,128)(2,1)} async-done(((bf16[1,96,32,128]{3,2,1,0:T(8,128)(2,1)}), bf16[4,96,32,128]{3,2,1,0:T(8,128)(2,1)}) %all-gather.4.cloned.1.call-update) | async-done | bytes 3145744 | tf_op jit(solution)/shard_map/all_gather | solution.py:182
  205.5 1.9 copy-done.10
  207.4 6.8 %shard_map.64 = s16[8,96,16,128]{3,2,1,0:T(8,128)(2,1)S(1)} custom-call(f32[3,96,128,128]{3,2,1,0:T(8,128)} %velocity_ref.5, bf16[4,96,32,128]{3,2,1,0:T(8,128)(2,1)S(1)} %copy-done.10, bf16[128,128]{1,0:T(8,128)(2,1)S(1)} %compare_convert_fusion.onehot_ref), custom_call_target="tpu_custom_call" | custom-call | flops 402653184 | bytes 12582912 | tf_op jit(solution)/shard_map/pallas_call | solution.py:46
  214.2 1.7 copy-done.2
  215.9 4.7 %all-to-all-start = ((s16[8,96,16,128]{3,2,1,0:T(8,128)(2,1)}), s16[8,96,16,128]{3,2,1,0:T(8,128)(2,1)}, u32[]{:S(2)}, u32[]{:S(2)}) async-start(s16[8,96,16,128]{3,2,1,0:T(8,128)(2,1)} %copy-done.2), calls=%async_computation | async-start | bytes 6291456 | tf_op jit(solution)/shard_map/all_to_all | solution.py:184
  221.0 1.3 copy-done.4
  222.3 1.3 copy-done.6
  223.5 1.9 copy-done.12
  225.4 18.9 %shard_map.67.rest_0_ = f32[36864,128]{1,0:T(8,128)} custom-call(s16[768,16,128]{2,1,0:T(8,128)(2,1)S(1)} %bitcast.21, f32[2,384,1]{2,1,0:T(8,128)S(1)} %copy.26.rates_ref, f32[16,128]{1,0:T(8,128)S(1)} %broadcast_add_fusion.shifts_ref, f32[2,384,384]{2,1,0:T(8,128)S(1)} %copy-done.4, f32[2,384,384]{2,1,0:T(8,128)S(1)} %copy-done.6), custom_call_target="tpu_custom_call" | custom-call | flops 7247757312 | bytes 9437184 | tf_op jit(solution)/shard_map/pallas_call | solution.py:132
  244.3 18.9 %shard_map.68.rest_0_ = f32[36864,128]{1,0:T(8,128)} custom-call(s16[768,16,128]{2,1,0:T(8,128)(2,1)S(1)} %bitcast.20, f32[2,384,1]{2,1,0:T(8,128)S(1)} %copy.26.rates_ref, f32[16,128]{1,0:T(8,128)S(1)} %broadcast_add_fusion.shifts_ref, f32[2,384,384]{2,1,0:T(8,128)S(1)} %copy-done.4, f32[2,384,384]{2,1,0:T(8,128)S(1)} %copy-done.6, ...), custom_call_target="tpu_custom_call", output_to_operand_aliasing={{}: (5, {})} | custom-call | flops 7247757312 | bytes 9437184 | tf_op jit(solution)/shard_map/pallas_call | solution.py:132
  263.1 1.3 copy-done.5
  264.4 1.3 copy-done.7
  265.7 20.9 %shard_map.69 = f32[36864,128]{1,0:T(8,128)} custom-call(s16[768,16,128]{2,1,0:T(8,128)(2,1)} %bitcast.4.values_ref, f32[2,384,1]{2,1,0:T(8,128)S(1)} %copy.26.rates_ref, f32[16,128]{1,0:T(8,128)S(1)} %broadcast_add_fusion.shifts_ref, f32[2,384,384]{2,1,0:T(8,128)S(1)} %copy-done.5, f32[2,384,384]{2,1,0:T(8,128)S(1)} %copy-done.7, ...), custom_call_target="tpu_custom_call", output_to_operand_aliasing={{}: (5, {})} | custom-call | flops 7247757312 | bytes 9437184 | tf_op jit(solution)/shard_map/pallas_call | solution.py:132
  (43 shorter events, 1.9 us)
Async XLA Ops:
  6.5 1.7 copy-start
  6.5 71.5 %all-gather.8.cloned.1.call-start = ((), (), s32[]{:S(2)}) async-start(), calls=%async_computation.5 | async-start | bytes 3932160 | tf_op jit(solution)/shard_map/all_gather | solution.py:182
  10.5 2.9 copy-start.15
  10.5 4.2 %copy-start.14 = (s32[16]{0:T(128)S(1)}, s32[16]{0:T(128)}, u32[]{:S(2)}) copy-start(s32[16]{0:T(128)} %param.8) | copy-start | bytes 196
  11.7 130.1 %all-gather.6.cloned.1.call-start = ((), (), s32[]{:S(2)}) async-start(), calls=%async_computation.4 | async-start | bytes 3932160 | tf_op jit(solution)/shard_map/all_gather | solution.py:182
  78.0 1.9 copy-start.9
  87.9 64.3 %all-to-all-start.2 = ((s16[8,96,16,128]{3,2,1,0:T(8,128)(2,1)}), s16[8,96,16,128]{3,2,1,0:T(8,128)(2,1)S(1)}, u32[]{:S(2)}, u32[]{:S(2)}) async-start(s16[8,96,16,128]{3,2,1,0:T(8,128)(2,1)} %shard_map.66), calls=%async_computation.2 | async-start | bytes 6291456 | tf_op jit(solution)/shard_map/all_to_all | solution.py:184
  91.6 114.0 %all-gather.4.cloned.1.call-start = ((), (), s32[]{:S(2)}) async-start(), calls=%async_computation.3 | async-start | bytes 3932160 | tf_op jit(solution)/shard_map/all_gather | solution.py:182
  141.8 1.9 copy-start.8
  150.5 1.7 copy-start.3
  152.2 1.6 copy-start.11
  153.8 62.1 %all-to-all-start.1 = ((s16[8,96,16,128]{3,2,1,0:T(8,128)(2,1)}), s16[8,96,16,128]{3,2,1,0:T(8,128)(2,1)S(1)}, u32[]{:S(2)}, u32[]{:S(2)}) async-start(s16[8,96,16,128]{3,2,1,0:T(8,128)(2,1)} %copy-done.3), calls=%async_computation.1 | async-start | bytes 6291456 | tf_op jit(solution)/shard_map/all_to_all | solution.py:184
  205.5 1.9 copy-start.10
  214.2 1.7 copy-start.2
  215.9 4.8 %copy-start.13 = (f32[2,384]{1,0:T(2,128)S(1)}, f32[2,384]{1,0:T(2,128)}, u32[]{:S(2)}) copy-start(f32[2,384]{1,0:T(2,128)} %param.9) | copy-start | bytes 9220
  215.9 47.2 %all-to-all-start = ((s16[8,96,16,128]{3,2,1,0:T(8,128)(2,1)}), s16[8,96,16,128]{3,2,1,0:T(8,128)(2,1)}, u32[]{:S(2)}, u32[]{:S(2)}) async-start(s16[8,96,16,128]{3,2,1,0:T(8,128)(2,1)} %copy-done.2), calls=%async_computation | async-start | bytes 6291456 | tf_op jit(solution)/shard_map/all_to_all | solution.py:184
  221.0 1.3 copy-start.4
  222.3 1.3 copy-start.6
  223.5 1.9 copy-start.12
  263.1 1.3 copy-start.5
  264.4 1.3 copy-start.7
  265.7 20.9 %copy-start.1 = (bf16[16,3,96,256]{3,2,1,0:T(8,128)(2,1)S(1)}, bf16[16,3,96,256]{3,2,1,0:T(8,128)(2,1)}, u32[]{:S(2)}) copy-start(bf16[16,3,96,256]{3,2,1,0:T(8,128)(2,1)} %param.7) | copy-start | bytes 7077892
Sparse Core Ops, SparseCore 0:
  11.8 66.1 all-gather.7
  79.6 62.1 all-gather.5
  143.3 62.1 all-gather.3

commit v2 on v1

--- a/solution.py
+++ b/solution.py
@@ -29,10 +29,13 @@
     return jnp.where(level < 0.0, -size, size)
 
 
-def spread_kernel(steps, velocity_ref, blocks_ref, onehot_ref, out_ref):
+def spread_kernel(steps, count, velocity_ref, onehot_ref, *rest):
+    blocks_refs, out_ref = rest[:count], rest[-1]
     onehot = onehot_ref[...]
     for y in range(velocity_ref.shape[1]):
-        block = blocks_ref[:, y].reshape(onehot.shape[0], blocks_ref.shape[3])
+        block = jnp.concatenate(
+            [ref[:, y].reshape(-1, ref.shape[3]) for ref in blocks_refs], 0
+        )
         forcing = lax.dot_general(
             block, onehot, (((0,), (0,)), ((), ())), preferred_element_type=F32
         )
@@ -40,28 +43,30 @@
         out_ref[:, y] = code.reshape(out_ref.shape[0], out_ref.shape[2], out_ref.shape[3])
 
 
-def spread(component, velocity, blocks, onehot, row_count, steps, step):
+def spread(component, velocity, blocks, onehot, after, row_count, steps, step):
     _, y_count, x_count, z_count = velocity.shape
     x_local = x_count // row_count
     return pl.pallas_call(
-        functools.partial(spread_kernel, steps),
+        functools.partial(spread_kernel, steps, len(blocks)),
         grid=(y_count // step,),
         in_specs=[
             pl.BlockSpec((1, step, x_count, z_count), lambda i: (component, i, 0, 0)),
-            pl.BlockSpec(
-                (blocks.shape[0], step) + blocks.shape[2:], lambda i: (0, i, 0, 0)
-            ),
             pl.BlockSpec(onehot.shape, lambda i: (0, 0)),
-        ],
+        ]
+        + [
+            pl.BlockSpec((block.shape[0], step) + block.shape[2:], lambda i: (0, i, 0, 0))
+            for block in blocks
+        ]
+        + [pl.BlockSpec(token.shape, lambda i: (0, 0)) for token in after],
         out_specs=pl.BlockSpec((row_count, step, x_local, z_count), lambda i: (0, i, 0, 0)),
         out_shape=jax.ShapeDtypeStruct((row_count, y_count, x_local, z_count), S16),
         compiler_params=pltpu.CompilerParams(vmem_limit_bytes=40 * 2**20),
         cost_estimate=pl.CostEstimate(
             flops=2 * y_count * x_count * z_count * onehot.shape[0],
-            bytes_accessed=y_count * x_count * z_count * 6 + blocks.size * 2,
+            bytes_accessed=y_count * x_count * z_count * 12,
             transcendentals=0,
         ),
-    )(velocity, blocks, onehot)
+    )(velocity, onehot, *blocks, *after)
 
 
 def split(value):
@@ -81,7 +86,8 @@
 
 
 def solve_kernel(steps, width, values_ref, rates_ref, shifts_ref, to_ref, from_ref, *rest):
-    out_ref, folded = rest[-2:]
+    out_ref, token_ref, folded = rest[-3:]
+    token_ref[...] = jnp.zeros_like(token_ref)
     pair_count = to_ref.shape[1]
     x_count, z_count = shifts_ref.shape
     sign = jnp.where(pl.program_id(0) == 0, 1.0, -1.0).astype(F32)
@@ -133,15 +139,19 @@
         functools.partial(solve_kernel, steps, 4),
         grid=(2,),
         in_specs=specs,
-        out_specs=pl.BlockSpec(
-            (pair_count * x_count, z_count), lambda p: (component * 2 + p, 0)
-        ),
-        out_shape=jax.ShapeDtypeStruct((field_count * point_count * x_count, z_count), F32),
+        out_specs=[
+            pl.BlockSpec((pair_count * x_count, z_count), lambda p: (component * 2 + p, 0)),
+            pl.BlockSpec((8, z_count), lambda p: (0, 0)),
+        ],
+        out_shape=[
+            jax.ShapeDtypeStruct((field_count * point_count * x_count, z_count), F32),
+            jax.ShapeDtypeStruct((8, z_count), F32),
+        ],
         scratch_shapes=[pltpu.VMEM((pair_count * x_count, z_count), F32)],
         input_output_aliases=aliases,
         compiler_params=pltpu.CompilerParams(vmem_limit_bytes=48 * 2**20),
         cost_estimate=pl.CostEstimate(
-            flops=12 * point_count * pair_count * x_count * z_count,
+            flops=36 * point_count * pair_count * x_count * z_count,
             bytes_accessed=values.size * 6,
             transcendentals=0,
         ),
@@ -163,12 +173,16 @@
     swap = (
         lanes[:, None] == (lanes % kx_total * 2 + lanes // kx_total)[None, :]
     ).astype(BF16)
-    parts = jnp.einsum("bcyk,kl->cybl", forcing_blocks, swap, preferred_element_type=BF16)
-    parts = parts.reshape(field_count, y_count, 2 * block_count, kx_total)
-    targets = lax.all_gather(mode_index, "kz", axis=0, tiled=True)
+    targets = lax.all_gather(mode_index, "kz", axis=0, tiled=False)
     columns = jnp.arange(column_count, dtype=jnp.int32)
-    keys = (2 * targets[:, None] + jnp.arange(2, dtype=jnp.int32)[None, :]).reshape(-1)
-    onehot = (keys[:, None] == (2 * kz_base + columns)[None, :]).astype(BF16)
+    reim = jnp.arange(2, dtype=jnp.int32)
+
+    slots = min(8, block_count)
+    owners = targets // mode_count
+    alike = owners[:, :, None] == owners[:, None, :]
+    order = jnp.arange(block_count, dtype=jnp.int32)
+    ranks = jnp.sum((alike & (order[None, :] < order[:, None])[None]).astype(jnp.int32), 2)
+    fits = jnp.max(ranks) < slots
 
     kz_total = mode_count * kz_count
     kz_scaled = (kz_base + columns // 2).astype(F32) / kz_total
@@ -177,15 +191,64 @@
     shifts = 1.0 + (kx_scaled**2)[:, None] + (kz_scaled**2)[None, :]
     rates = eigen_rates[:, :, None]
 
-    result = None
-    for component in range(field_count):
-        blocks = lax.all_gather(parts[component], "kz", axis=0, tiled=False)
-        sent = spread(component, velocity, blocks, onehot, row_count, steps, 16)
-        values = lax.all_to_all(sent, "rows", split_axis=0, concat_axis=0, tiled=True)
-        values = values.reshape(row_count * y_count, kx_local, column_count)
-        result = solve(
-            component, field_count, values, rates, shifts, to_modes, from_modes, result, steps
-        )
+    def pipeline(send, keys):
+        onehot = (keys.reshape(-1)[:, None] == (2 * kz_base + columns)[None, :]).astype(BF16)
+        result = None
+        tokens = []
+        for component in range(field_count):
+            blocks = send(component)
+            sent = spread(
+                component, velocity, blocks, onehot, tokens[:-1][-1:], row_count, steps, 16
+            )
+            values = lax.all_to_all(sent, "rows", split_axis=0, concat_axis=0, tiled=True)
+            values = values.reshape(row_count * y_count, kx_local, column_count)
+            result, token = solve(
+                component, field_count, values, rates, shifts, to_modes, from_modes, result, steps
+            )
+            tokens.append(token)
+        return result
+
+    def some(_):
+        mine = lax.axis_index("kz")
+        places = jnp.arange(kz_count * slots, dtype=jnp.int32)
+        distances = (owners - mine + kz_count) % kz_count
+        wanted = lax.dynamic_index_in_dim(distances * slots + ranks, mine, 0, False)
+        select = (places[:, None] == wanted[None, :]).astype(BF16)
+        picked = jnp.einsum("pb,bcyk->pcyk", select, forcing_blocks, preferred_element_type=BF16)
+        parts = jnp.einsum("pcyk,kl->cypl", picked, swap, preferred_element_type=BF16)
+        parts = parts.reshape(field_count, y_count, kz_count, 2 * slots, kx_total)
+        parts = parts.transpose(0, 2, 1, 3, 4)
+        here = (owners == mine)[:, None, :] & (
+            ranks[:, None, :] == jnp.arange(slots, dtype=jnp.int32)[None, :, None]
+        )
+        modes = jnp.sum(jnp.where(here, targets[:, None, :] + 1, 0), 2) - 1
+        sources = (mine - jnp.arange(kz_count, dtype=jnp.int32) + kz_count) % kz_count
+        modes = modes[sources]
+        keys = jnp.where(modes[:, :, None] < 0, -1, 2 * modes[:, :, None] + reim)
+
+        def send(component):
+            return [parts[component, :1]] + [
+                lax.ppermute(
+                    parts[component, distance : distance + 1],
+                    "kz",
+                    [(source, (source + distance) % kz_count) for source in range(kz_count)],
+                )
+                for distance in range(1, kz_count)
+            ]
+
+        return pipeline(send, keys)
+
+    def every(_):
+        parts = jnp.einsum("bcyk,kl->cybl", forcing_blocks, swap, preferred_element_type=BF16)
+        parts = parts.reshape(field_count, y_count, 2 * block_count, kx_total)
+        keys = 2 * targets[:, :, None] + reim
+
+        def send(component):
+            return [lax.all_gather(parts[component], "kz", axis=0, tiled=False)]
+
+        return pipeline(send, keys)
+
+    result = lax.cond(fits, some, every, 0)
     return result.reshape(field_count, row_count * y_count, kx_local, column_count)
 
 

time: 294 us -> 294 us (level)
  the two profiles are of different devices: /device:TPU:0 before, /device:TPU:8 now
where the time goes in v2:
time: 294 us; the launch traced here: 299 us
  waiting for transfers between devices  148 us (50%)
  Pallas kernels  84.8 us (29%)
  local copies, waits for them, and re-layouts  19.4 us (7%)
  between operations  14.7 us (5%)
  starting transfers between devices  12.7 us (4%)
  blocking collectives  8.45 us (3%)
  loops' own time  7.58 us (3%)
    all_gather x3, waiting for transfers between devices, send(): return [lax.all_gather(parts[component], 'kz', axis=0, tiled=False)]  131 us
    pallas_call x3, Pallas kernels, solve(): pl.pallas_call(functools.partial(solve_kernel, steps, 4), grid=(2,), in_s...  61.1 us
    pallas_call x3, Pallas kernels, spread(): pl.pallas_call(functools.partial(spread_kernel, steps, len(blocks)), grid...  23.7 us
    all_to_all x3, waiting for transfers between devices, pipeline(): lax.all_to_all(sent, 'rows', split_axis=0, concat_axis=0, tiled=True)  16.7 us
    all_to_all x3, starting transfers between devices, pipeline(): lax.all_to_all(sent, 'rows', split_axis=0, concat_axis=0, tiled=True)  12.6 us
    slice x7, local copies, waits for them, and re-layouts, send(): return [lax.all_gather(parts[component], 'kz', axis=0, tiled=False)]  8.87 us
    unnamed x1, blocking collectives  8.45 us
    another operation x1, loops' own time, shards(): result = lax.cond(fits, some, every, 0)  7.58 us
  transfers between devices with their start and end apart: 6, of which 4 were waited for; matrix products, arithmetic and copies ran while one was open for 2% of the time, Pallas kernels for 22%

profile of v2, /device:TPU:8, one launch (start us, length us, event | category | flops | bytes accessed | tf_op | source)
XLA Modules:
  0.0 299.5 jit_solution(6635916069499659163)
XLA Ops:
  6.6 1.2 dynamic-slice
  8.5 0.9 dynamic-update-slice
  9.4 8.4 %all-reduce = s32[64]{0:T(128)S(1)} all-reduce(s32[64]{0:T(128)S(1)} %dynamic-update-slice), channel_id=2, replica_groups=mesh['rows'=8,'kz'=4] {'kz'}, use_global_device_ids=true, to_apply=%add | all-reduce | flops 64 | bytes 512
  18.2 0.6 iota.61
  18.8 0.6 reduce_max.9
  20.1 272.6 %conditional.1 = (f32[3,768,16,128]{3,2,1,0:T(8,128)}) conditional(s32[]{:T(128)} %convert_element_type.33, (s32[4,16]{1,0:T(4,128)S(1)}, s32[2]{0:T(128)S(1)}, s32[]{:T(128)}, s32[128]{0:T(128)S(1)}, bf16[256,256]{1,0:T(8,128)(2,1)S(1)}, /*index=5*/bf16[16,3,96,256]{3,2,1,0:T(8,128)(2,1)}, f32[3,96,128,128]{3,2,1,0:T(8,128)}, ...), branch_computations={%region_2.3_spmd, %region_3.5_spmd} | conditional | flops 67117273088 | bytes 205535968 | solution.py:251
  20.2 2.4 convolution_bitcast_fusion
  22.6 1.1 fusion.29
  23.7 0.4 copy.39
  24.1 1.1 slice.39
  25.3 0.4 copy.40
  25.8 1.1 slice.41
  27.3 58.5 %all-gather.7.cloned.1.call-done.rest_0_ = bf16[4,96,32,128]{3,2,1,0:T(8,128)(2,1)} async-done(((bf16[1,96,32,128]{3,2,1,0:T(8,128)(2,1)}), bf16[4,96,32,128]{3,2,1,0:T(8,128)(2,1)}) %all-gather.7.cloned.1.call-update) | async-done | bytes 3145744 | tf_op jit(solution)/shard_map/cond/branch_0_fun/all_gather | solution.py:247
  85.8 1.9 copy-done.1
  87.6 7.9 %branch_0_fun.6 = s16[8,96,16,128]{3,2,1,0:T(8,128)(2,1)} custom-call(f32[3,96,128,128]{3,2,1,0:T(8,128)} %get-tuple-element.56.velocity_ref, bf16[128,128]{1,0:T(8,128)(2,1)S(1)} %compare_convert_fusion.onehot_ref, bf16[4,96,32,128]{3,2,1,0:T(8,128)(2,1)S(1)} %copy-done.1), custom_call_target="tpu_custom_call" | custom-call | flops 402653184 | bytes 18874368 | tf_op jit(solution)/shard_map/cond/branch_0_fun/pallas_call | solution.py:49
  95.5 3.7 %all-to-all-start.3 = ((s16[8,96,16,128]{3,2,1,0:T(8,128)(2,1)}), s16[8,96,16,128]{3,2,1,0:T(8,128)(2,1)S(1)}, u32[]{:S(2)}, u32[]{:S(2)}) async-start(s16[8,96,16,128]{3,2,1,0:T(8,128)(2,1)} %branch_0_fun.6), calls=%async_computation.3 | async-start | bytes 6291456 | tf_op jit(solution)/shard_map/cond/branch_0_fun/all_to_all | solution.py:203
  99.3 2.5 copy.38
  101.8 2.1 slice.37
  103.9 45.6 %all-gather.9.cloned.1.call-done.rest_0_ = bf16[4,96,32,128]{3,2,1,0:T(8,128)(2,1)} async-done(((bf16[1,96,32,128]{3,2,1,0:T(8,128)(2,1)}), bf16[4,96,32,128]{3,2,1,0:T(8,128)(2,1)}) %all-gather.9.cloned.1.call-update) | async-done | bytes 3145744 | tf_op jit(solution)/shard_map/cond/branch_0_fun/all_gather | solution.py:247
  149.5 1.9 copy-done
  151.4 7.9 %branch_0_fun.9 = s16[8,96,16,128]{3,2,1,0:T(8,128)(2,1)} custom-call(f32[3,96,128,128]{3,2,1,0:T(8,128)} %get-tuple-element.56.velocity_ref, bf16[128,128]{1,0:T(8,128)(2,1)S(1)} %compare_convert_fusion.onehot_ref, bf16[4,96,32,128]{3,2,1,0:T(8,128)(2,1)S(1)} %copy-done), custom_call_target="tpu_custom_call" | custom-call | flops 402653184 | bytes 18874368 | tf_op jit(solution)/shard_map/cond/branch_0_fun/pallas_call | solution.py:49
  159.3 4.6 %all-to-all-start.5 = ((s16[8,96,16,128]{3,2,1,0:T(8,128)(2,1)}), s16[8,96,16,128]{3,2,1,0:T(8,128)(2,1)}, u32[]{:S(2)}, u32[]{:S(2)}) async-start(s16[8,96,16,128]{3,2,1,0:T(8,128)(2,1)} %branch_0_fun.9), calls=%async_computation.5 | async-start | bytes 6291456 | tf_op jit(solution)/shard_map/cond/branch_0_fun/all_to_all | solution.py:203
  163.9 0.9 copy.44.rates_ref
  164.9 1.0 copy-done.6
  165.9 20.0 %branch_0_fun.7 = (f32[36864,128]{1,0:T(8,128)}, f32[8,128]{1,0:T(8,128)S(1)}) custom-call(s16[768,16,128]{2,1,0:T(8,128)(2,1)S(1)} %bitcast.70, f32[2,384,1]{2,1,0:T(8,128)S(1)} %copy-done.6, f32[16,128]{1,0:T(8,128)S(1)} %get-tuple-element.64.shifts_ref, f32[2,384,384]{2,1,0:T(8,128)} %get-tuple-element.65.to_ref, f32[2,384,384]{2,1,0:T(8,128)} %get-tuple-element.66.from_ref), custom_call_target="tpu_custom_call" | custom-call | flops 21743271936 | bytes 9437184 | tf_op jit(solution)/shard_map/cond/branch_0_fun/pallas_call | solution.py:138
  185.9 27.3 %all-gather.5.cloned.1.call-done.rest_0_ = bf16[4,96,32,128]{3,2,1,0:T(8,128)(2,1)} async-done(((bf16[1,96,32,128]{3,2,1,0:T(8,128)(2,1)}), bf16[4,96,32,128]{3,2,1,0:T(8,128)(2,1)}) %all-gather.5.cloned.1.call-update) | async-done | bytes 3145744 | tf_op jit(solution)/shard_map/cond/branch_0_fun/all_gather | solution.py:247
  213.3 1.9 copy-done.2
  215.2 7.9 %branch_0_fun.8 = s16[8,96,16,128]{3,2,1,0:T(8,128)(2,1)} custom-call(f32[3,96,128,128]{3,2,1,0:T(8,128)} %get-tuple-element.56.velocity_ref, bf16[128,128]{1,0:T(8,128)(2,1)S(1)} %compare_convert_fusion.onehot_ref, bf16[4,96,32,128]{3,2,1,0:T(8,128)(2,1)S(1)} %copy-done.2, f32[8,128]{1,0:T(8,128)S(1)} %get-tuple-element.67.rest_1_), custom_call_target="tpu_custom_call" | custom-call | flops 402653184 | bytes 18874368 | tf_op jit(solution)/shard_map/cond/branch_0_fun/pallas_call | solution.py:49
  223.1 4.3 %all-to-all-start.4 = ((s16[8,96,16,128]{3,2,1,0:T(8,128)(2,1)}), s16[8,96,16,128]{3,2,1,0:T(8,128)(2,1)S(1)}, u32[]{:S(2)}, u32[]{:S(2)}) async-start(s16[8,96,16,128]{3,2,1,0:T(8,128)(2,1)} %branch_0_fun.8), calls=%async_computation.4 | async-start | bytes 6291456 | tf_op jit(solution)/shard_map/cond/branch_0_fun/all_to_all | solution.py:203
  227.4 21.1 %branch_0_fun.10 = (f32[36864,128]{1,0:T(8,128)}, f32[8,128]{1,0:T(8,128)}) custom-call(s16[768,16,128]{2,1,0:T(8,128)(2,1)} %bitcast.5.values_ref, f32[2,384,1]{2,1,0:T(8,128)S(1)} %copy-done.7, f32[16,128]{1,0:T(8,128)S(1)} %copy-done.10, f32[2,384,384]{2,1,0:T(8,128)} %get-tuple-element.65.to_ref, ...), custom_call_target="tpu_custom_call", output_to_operand_aliasing={{0}: (5, {})} | custom-call | flops 21743271936 | bytes 9437184 | tf_op jit(solution)/shard_map/cond/branch_0_fun/pallas_call | solution.py:138
  248.5 16.7 %all-to-all-done.4 = s16[8,96,16,128]{3,2,1,0:T(8,128)(2,1)S(1)} async-done(((s16[8,96,16,128]{3,2,1,0:T(8,128)(2,1)}), s16[8,96,16,128]{3,2,1,0:T(8,128)(2,1)S(1)}, u32[]{:S(2)}, u32[]{:S(2)}) %all-to-all-start.4) | async-done | bytes 3145760 | tf_op jit(solution)/shard_map/cond/branch_0_fun/all_to_all | solution.py:203
  265.2 20.0 %branch_0_fun.11 = (f32[36864,128]{1,0:T(8,128)}, f32[8,128]{1,0:T(8,128)}) custom-call(s16[768,16,128]{2,1,0:T(8,128)(2,1)S(1)} %bitcast.71, f32[2,384,1]{2,1,0:T(8,128)S(1)} %copy-done.7, f32[16,128]{1,0:T(8,128)S(1)} %copy-done.10, f32[2,384,384]{2,1,0:T(8,128)} %get-tuple-element.65.to_ref, ...), custom_call_target="tpu_custom_call", output_to_operand_aliasing={{0}: (5, {})} | custom-call | flops 21743271936 | bytes 9437184 | tf_op jit(solution)/shard_map/cond/branch_0_fun/pallas_call | solution.py:138
  (38 shorter events, 1.0 us)
Async XLA Ops:
  20.1 144.8 %copy-start.9 = (f32[16,128]{1,0:T(8,128)}, f32[16,128]{1,0:T(8,128)S(1)}, u32[]{:S(2)}) copy-start(f32[16,128]{1,0:T(8,128)S(1)} %get-tuple-element.64.shifts_ref) | copy-start | bytes 24580 | tf_op jit(solution)/shard_map/cond
  20.1 65.7 %all-gather.7.cloned.1.call-start = ((), (), s32[]{:S(2)}) async-start(), calls=%async_computation.7 | async-start | bytes 3932160 | tf_op jit(solution)/shard_map/cond/branch_0_fun/all_gather | solution.py:247
  25.3 124.2 %all-gather.9.cloned.1.call-start = ((), (), s32[]{:S(2)}) async-start(), calls=%async_computation.8 | async-start | bytes 3932160 | tf_op jit(solution)/shard_map/cond/branch_0_fun/all_gather | solution.py:247
  85.8 1.9 copy-start.1
  95.5 63.8 %all-to-all-start.3 = ((s16[8,96,16,128]{3,2,1,0:T(8,128)(2,1)}), s16[8,96,16,128]{3,2,1,0:T(8,128)(2,1)S(1)}, u32[]{:S(2)}, u32[]{:S(2)}) async-start(s16[8,96,16,128]{3,2,1,0:T(8,128)(2,1)} %branch_0_fun.6), calls=%async_computation.3 | async-start | bytes 6291456 | tf_op jit(solution)/shard_map/cond/branch_0_fun/all_to_all | solution.py:203
  99.2 114.0 %all-gather.5.cloned.1.call-start = ((), (), s32[]{:S(2)}) async-start(), calls=%async_computation.6 | async-start | bytes 3932160 | tf_op jit(solution)/shard_map/cond/branch_0_fun/all_gather | solution.py:247
  149.5 1.9 copy-start
  159.3 4.6 %copy-start.8 = (f32[2,384,1]{1,0,2:T(2,128)S(1)}, f32[2,384,1]{1,0,2:T(2,128)}, u32[]{:S(2)}) copy-start(f32[2,384,1]{1,0,2:T(2,128)} %get-tuple-element.168) | copy-start | bytes 9220 | tf_op jit(solution)/shard_map/cond
  159.3 63.8 %all-to-all-start.5 = ((s16[8,96,16,128]{3,2,1,0:T(8,128)(2,1)}), s16[8,96,16,128]{3,2,1,0:T(8,128)(2,1)}, u32[]{:S(2)}, u32[]{:S(2)}) async-start(s16[8,96,16,128]{3,2,1,0:T(8,128)(2,1)} %branch_0_fun.9), calls=%async_computation.5 | async-start | bytes 6291456 | tf_op jit(solution)/shard_map/cond/branch_0_fun/all_to_all | solution.py:203
  164.9 1.0 copy-start.6
  213.3 1.9 copy-start.2
  223.1 4.3 %copy-start.7 = (f32[2,384,1]{2,1,0:T(8,128)S(1)}, f32[2,384,1]{2,1,0:T(8,128)}, u32[]{:S(2)}) copy-start(f32[2,384,1]{2,1,0:T(8,128)} %copy.44.rates_ref) | copy-start | bytes 9220 | tf_op jit(solution)/shard_map/cond
  223.1 4.3 %copy-start.10 = (f32[16,128]{1,0:T(8,128)S(1)}, f32[16,128]{1,0:T(8,128)}, u32[]{:S(2)}) copy-start(f32[16,128]{1,0:T(8,128)} %copy-done.9) | copy-start | bytes 24580 | tf_op jit(solution)/shard_map/cond
  223.1 42.1 %all-to-all-start.4 = ((s16[8,96,16,128]{3,2,1,0:T(8,128)(2,1)}), s16[8,96,16,128]{3,2,1,0:T(8,128)(2,1)S(1)}, u32[]{:S(2)}, u32[]{:S(2)}) async-start(s16[8,96,16,128]{3,2,1,0:T(8,128)(2,1)} %branch_0_fun.8), calls=%async_computation.4 | async-start | bytes 6291456 | tf_op jit(solution)/shard_map/cond/branch_0_fun/all_to_all | solution.py:203
Sparse Core Ops, SparseCore 0:
  25.4 60.2 all-gather.6
  87.3 62.1 all-gather.8
  151.1 62.1 all-gather.4
